TPU v7x, 32 devices: a whole 2x2x4 slice. The times are simulated.
32 devices in a mesh: ctx: 8 (over y, x, core), seq: 4 (over z).
Axes of the slice: x: 2, y: 2, z: 4, core: 2. Of those that a mesh axis runs over, the one named last changes fastest.
Arguments:
- lin_query: bfloat16 [2048, 4096], P(('seq', 'ctx')), parts along dimension 0, may hold values from -6 to 6
- lin_keys: bfloat16 [2048, 1024], P(('seq', 'ctx')), parts along dimension 0, may hold values from -6 to 6
- lin_values: bfloat16 [2048, 1024], P(('seq', 'ctx')), parts along dimension 0, may hold values from -6 to 6
- state_in: float32 [32, 128, 128], P('seq'), parts along dimension 0, may hold values from -256 to 256
- norm_gain: float32 [4096], replicated, may hold values from 0.1 to 1.9
- soft_query: bfloat16 [2048, 4096], P(('seq', 'ctx')), parts along dimension 0, may hold values from -7 to 7
- soft_keys: bfloat16 [2048, 1024], P(('seq', 'ctx')), parts along dimension 0, may hold values from -7 to 7
- soft_values: bfloat16 [2048, 1024], P(('seq', 'ctx')), parts along dimension 0, may hold values from -6 to 6
Outputs:
- lin_out: bfloat16 [2048, 4096], P(('seq', 'ctx')), parts along dimension 0
- state_out: float32 [32, 128, 128], P('seq'), parts along dimension 0
- soft_out: bfloat16 [2048, 4096], P(('seq', 'ctx')), parts along dimension 0
There are 4 independent parts, one for each index of `seq`. A program takes and returns all parts, laid end to end along the dimension named above; an argument that names none is the same for every part. Nothing has to cross between parts.
All inputs are finite; a program needn't handle non-finite values.
Results may differ from a plain program's by a relative error of at most 0.014.
Values may be sent and summed in bfloat16 or wider, within the bound.
A program may use at most 64 MiB of HBM per device.

v0:
```python
import jax
import jax.numpy as jnp
from jax import lax
from jax.sharding import PartitionSpec as P


def prefix_2(value, axis, join, neutral):
    count, mine = (lax.axis_size(axis), lax.axis_index(axis))
    pieces = lax.all_gather(value, axis)
    so_far = jnp.full_like(value, 0) + jnp.asarray(neutral, value.dtype)

    def step(position, so_far):
        longer = join(so_far, pieces[position])
        return jnp.where(position < mine, longer, so_far)

    return lax.fori_loop(0, count - 1, step, so_far)


def add_states(earlier, later):
    return earlier + later


def linear_blocks(query, keys, values, state):
    total = query.shape[0]
    block = min(512, total)
    steps = total // block
    heads = query.shape[1]
    width = query.shape[2]
    q_blocks = query.reshape(steps, block, heads, width)
    k_blocks = keys.reshape(steps, block, heads, width)
    v_blocks = values.reshape(steps, block, heads, width)
    lower = jnp.tril(jnp.ones((block, block), jnp.float32))

    def advance(memory, pieces):
        q_block, k_block, v_block = pieces
        carried = jnp.einsum(
            "thd,hde->the", q_block.astype(jnp.float32), memory, precision=lax.Precision.HIGHEST
        )
        inner_scores = (
            jnp.einsum("thd,shd->hts", q_block, k_block, preferred_element_type=jnp.float32) * lower
        )
        inner = jnp.einsum(
            "hts,she->the",
            inner_scores,
            v_block.astype(jnp.float32),
            precision=lax.Precision.HIGHEST,
        )
        update = jnp.einsum("thd,the->hde", k_block, v_block, preferred_element_type=jnp.float32)
        return (memory + update, carried + inner)

    final, outputs = lax.scan(advance, state, (q_blocks, k_blocks, v_blocks))
    return (outputs.reshape(total, heads, width), final)


def head_norm(raw, gain):
    square = jnp.mean(raw * raw, axis=-1, keepdims=True)
    return (raw * lax.rsqrt(square + 1e-06) * gain).astype(jnp.bfloat16)


def causal_softmax(pieces):
    query, keys, values = pieces
    total = query.shape[0]
    heads = query.shape[1]
    width = query.shape[2]
    block = min(512, total)
    steps = total // block
    scale = width ** (-0.5)
    q_blocks = query.reshape(steps, block, heads, width)
    key_pos = jnp.arange(total, dtype=jnp.int32)

    def one_block(parts):
        q_block, offset = parts
        scores = (
            jnp.einsum("qmd,kmd->mqk", q_block, keys, preferred_element_type=jnp.float32) * scale
        )
        query_pos = offset + jnp.arange(block, dtype=jnp.int32)
        allowed = key_pos[None, None, :] <= query_pos[None, :, None]
        scores = jnp.where(allowed, scores, -1e30)
        top = jnp.max(scores, axis=-1, keepdims=True)
        expo = jnp.exp(scores - top)
        weights = (expo / jnp.sum(expo, axis=-1, keepdims=True)).astype(jnp.bfloat16)
        return jnp.einsum(
            "mqk,kmd->qmd", weights, values, preferred_element_type=jnp.float32
        ).astype(jnp.bfloat16)

    offsets = jnp.arange(steps, dtype=jnp.int32) * block
    outputs = lax.map(one_block, (q_blocks, offsets))
    return outputs.reshape(total, heads, width)


def shards(
    lin_query, lin_keys, lin_values, state_in, norm_gain, soft_query, soft_keys, soft_values
):
    rows = lin_query.shape[0]
    kv_heads = state_in.shape[0]
    head_dim = state_in.shape[1]
    heads = lin_query.shape[1] // head_dim
    group = heads // kv_heads
    split = (rows, heads, head_dim)
    shared = (rows, kv_heads, head_dim)
    gain = norm_gain.reshape(heads, head_dim)
    query = lin_query.reshape(split)
    keys = lin_keys.reshape(shared)
    values = lin_values.reshape(shared)
    wide_keys = jnp.repeat(keys, group, axis=1)
    wide_values = jnp.repeat(values, group, axis=1)
    local_state = jnp.einsum("thd,the->hde", keys, values, preferred_element_type=jnp.float32)
    prefix = prefix_2(local_state, "ctx", add_states, jnp.zeros_like(local_state))
    before = jnp.repeat(state_in + prefix, group, axis=0)
    raw, ending = linear_blocks(query, wide_keys, wide_values, before)
    lin_out = head_norm(raw, gain).reshape(rows, heads * head_dim)
    state_out = state_in + lax.psum(local_state.astype(jnp.bfloat16), "ctx").astype(jnp.float32)
    soft_input = (soft_query.astype(jnp.float32) + lin_out.astype(jnp.float32)).astype(jnp.bfloat16)
    soft_k = jnp.repeat(soft_keys.reshape(shared), group, axis=1)
    soft_v = jnp.repeat(soft_values.reshape(shared), group, axis=1)
    attended = causal_softmax(
        (
            lax.all_to_all(
                soft_input.reshape(split), "ctx", split_axis=1, concat_axis=0, tiled=True
            ),
            lax.all_to_all(soft_k, "ctx", split_axis=1, concat_axis=0, tiled=True),
            lax.all_to_all(soft_v, "ctx", split_axis=1, concat_axis=0, tiled=True),
        )
    )
    soft_out = lax.all_to_all(attended, "ctx", split_axis=0, concat_axis=1, tiled=True).reshape(
        rows, heads * head_dim
    )
    return (lin_out, state_out, soft_out)


def solution(mesh):
    in_specs = (
        P(("seq", "ctx"), None),
        P(("seq", "ctx"), None),
        P(("seq", "ctx"), None),
        P("seq", None, None),
        P(),
        P(("seq", "ctx"), None),
        P(("seq", "ctx"), None),
        P(("seq", "ctx"), None),
    )
    out_specs = (P(("seq", "ctx"), None), P("seq", None, None), P(("seq", "ctx"), None))
    return jax.shard_map(shards, mesh=mesh, in_specs=in_specs, out_specs=out_specs, check_vma=False)
```

profile of v0, /device:TPU:0, one launch (start us, length us, event | category | flops | bytes accessed | tf_op | source)
XLA Modules:
  0.0 168.5 jit_solution(18187493341674480513)
XLA Ops:
  7.2 0.0 copy-start
  7.2 0.0 copy-start.2
  7.2 0.0 copy-start.3
  7.2 0.0 all-gather.3.cloned.1.call-start
  7.2 2.2 %fusion.21 = (bf16[8,128,128]{2,1,0:T(8,128)(2,1)}, f32[8,128,128]{2,1,0:T(8,128)}) fusion(bf16[64,1024]{1,0:T(8,128)(2,1)} %param.12, bf16[64,1024]{1,0:T(8,128)(2,1)} %param.11), kind=kOutput, calls=%fused_computation.40 | convolution fusion | flops 16908288 | bytes 1048576 | tf_op jit(solution)/shard_map/thd,the->hde/dot_general | solution.py:107
  9.4 0.0 all-gather.3.cloned.1.call-update
  9.5 0.9 copy_bitcast_fusion.3
  10.4 0.9 broadcast_in_dim.67
  11.3 5.2 %all-to-all-start.1 = ((bf16[64,32,128]{2,0,1:T(8,128)(2,1)}), bf16[64,32,128]{2,0,1:T(8,128)(2,1)}, u32[]{:S(2)}, u32[]{:S(2)}) async-start(bf16[64,32,128]{2,0,1:T(8,128)(2,1)} %bitcast.10), calls=%async_computation.1 | async-start | bytes 1048576 | tf_op jit(solution)/shard_map/all_to_all | solution.py:121
  16.5 0.0 all-reduce.2.cloned.1.call-start
  16.5 0.7 all-reduce.2.cloned.1.call-update
  17.2 0.9 copy_bitcast_fusion.5
  18.2 0.0 copy-done.2
  18.2 0.0 copy-done.3
  18.3 0.1 broadcast_in_dim.62
  18.4 0.0 copy-done
  18.4 0.4 convolution_multiply_fusion
  18.8 0.0 copy-start.1
  18.8 33.4 %all-gather.3.cloned.1.call-done = f32[64,128,128]{2,1,0:T(8,128)} async-done(((f32[8,128,128]{2,1,0:T(8,128)}), f32[64,128,128]{2,1,0:T(8,128)}) %all-gather.3.cloned.1.call-update) | async-done | bytes 4194320 | tf_op jit(solution)/shard_map/all_gather | solution.py:9
  52.2 8.7 %while.9 = (s32[]{:T(128)}, f32[8,128,128]{2,1,0:T(8,128)S(1)}, s32[]{:T(128)}, f32[8,8,128,128]{3,2,1,0:T(8,128)}, s32[]{:T(128)}, /*index=5*/s32[]{:T(128)}) while((s32[]{:T(128)}, f32[8,128,128]{2,1,0:T(8,128)S(1)}, s32[]{:T(128)}, f32[8,8,128,128]{3,2,1,0:T(8,128)}, s32[]{:T(128)}, /*index=5*/s32[]{:T(128)}) %tuple.52), condition=%wide.region_1.2_spmd.clone, body=%wide.region_0.1_spmd.clone.sunk | while | flops 393220 | bytes 1572957 | solution.py:16
  52.2 1.2 add_select_fusion.2
  53.4 1.2 add_select_fusion.2
  54.7 1.2 add_select_fusion.2
  55.9 1.2 add_select_fusion.2
  57.2 1.2 add_select_fusion.2
  58.4 1.2 add_select_fusion.2
  59.7 1.2 add_select_fusion.2
  60.9 48.4 %all-reduce.2.cloned.1.call-done = bf16[8,128,128]{2,1,0:T(8,128)(2,1)} async-done(((bf16[8,128,128]{2,1,0:T(8,128)(2,1)}), bf16[8,128,128]{2,1,0:T(8,128)(2,1)}) %all-reduce.2.cloned.1.call-update) | async-done | bytes 262160 | tf_op jit(solution)/shard_map/psum | solution.py:112
  109.4 0.0 copy-done.1
  109.4 1.8 %convert_add_fusion = (f32[8,128,128]{2,1,0:T(8,128)}, f32[8,128,128]{2,1,0:T(8,128)S(1)}) fusion(f32[8,128,128]{2,1,0:T(8,128)S(1)} %copy-done.1, bf16[8,128,128]{2,1,0:T(8,128)(2,1)} %all-reduce.2.cloned.1.call-done, f32[8,128,128]{2,1,0:T(8,128)S(1)} %get-tuple-element.121), kind=kLoop, calls=%fused_computation.26 | loop fusion | flops 393216 | bytes 2359296 | tf_op jit(solution)/shard_map/add | solution.py:112
  111.2 0.2 broadcast_in_dim.61
  111.5 0.0 copy-start.4
  111.5 1.1 convolution_bitcast_fusion
  112.6 0.1 broadcast_in_dim.65
  112.7 1.0 multiply_reduce_fusion
  113.7 0.0 all-to-all-done.1
  113.7 0.9 broadcast_in_dim.69
  114.6 3.5 %all-to-all-start.2 = ((bf16[64,32,128]{2,0,1:T(8,128)(2,1)}), bf16[64,32,128]{2,0,1:T(8,128)(2,1)S(1)}, u32[]{:S(2)}, u32[]{:S(2)}) async-start(bf16[64,32,128]{2,0,1:T(8,128)(2,1)} %bitcast.14), calls=%async_computation.2 | async-start | bytes 1048576 | tf_op jit(solution)/shard_map/all_to_all | solution.py:122
  118.1 0.0 copy-done.4
  118.1 2.2 %fusion.10 = (bf16[8,32,8,128]{3,2,1,0:T(8,128)(2,1)S(1)}, bf16[64,4096]{1,0:T(8,128)(2,1)}) fusion(bf16[64,4096]{1,0:T(8,128)(2,1)} %param.15, f32[64,32,128]{2,0,1:T(8,128)S(1)} %get-tuple-element.152, f32[32,128]{1,0:T(8,128)S(1)} %bitcast.108, f32[64,32]{0,1:T(8,128)S(1)} %add_rsqrt_fusion), kind=kLoop, calls=%fused_computation.21 | loop fusion | flops 1835008 | bytes 2646016
  120.3 0.9 copy.75
  121.3 6.5 %all-to-all-done.2 = bf16[64,32,128]{2,0,1:T(8,128)(2,1)S(1)} async-done(((bf16[64,32,128]{2,0,1:T(8,128)(2,1)}), bf16[64,32,128]{2,0,1:T(8,128)(2,1)S(1)}, u32[]{:S(2)}, u32[]{:S(2)}) %all-to-all-start.2) | async-done | bytes 524320 | tf_op jit(solution)/shard_map/all_to_all | solution.py:122
  127.8 3.5 %all-to-all-start = ((bf16[64,32,128]{2,0,1:T(8,128)(2,1)}), bf16[64,32,128]{2,0,1:T(8,128)(2,1)S(1)}, u32[]{:S(2)}, u32[]{:S(2)}) async-start(bf16[64,32,128]{2,0,1:T(8,128)(2,1)} %bitcast.95), calls=%async_computation | async-start | bytes 1048576 | tf_op jit(solution)/shard_map/all_to_all | solution.py:118
  131.3 0.1 iota_compare_fusion
  131.4 1.1 copy.40
  132.5 8.5 %all-to-all-done = bf16[64,32,128]{2,0,1:T(8,128)(2,1)S(1)} async-done(((bf16[64,32,128]{2,0,1:T(8,128)(2,1)}), bf16[64,32,128]{2,0,1:T(8,128)(2,1)S(1)}, u32[]{:S(2)}, u32[]{:S(2)}) %all-to-all-start) | async-done | bytes 524320 | tf_op jit(solution)/shard_map/all_to_all | solution.py:118
  141.0 3.6 %fusion.22 = (f32[4,512]{1,0:T(4,128)S(1)}, f32[4,512,512]{1,2,0:T(8,128)}) fusion(pred[512,512]{0,1:T(8,128)(4,1)S(1)} %iota_compare_fusion, bf16[512,4,128]{2,0,1:T(8,128)(2,1)S(1)} %bitcast.107, bf16[512,4,128]{2,0,1:T(8,128)(2,1)S(1)} %bitcast.106), kind=kOutput, calls=%fused_computation.41 | convolution fusion | flops 272630272 | bytes 5513216 | tf_op jit(solution)/shard_map/while/body/eval_jaxpr/sub | solution.py:80
  144.6 3.1 %fusion.8 = bf16[512,4,128]{2,0,1:T(8,128)(2,1)S(1)} fusion(bf16[512,4,128]{2,0,1:T(8,128)(2,1)S(1)} %bitcast.105, f32[4,512,512]{1,2,0:T(8,128)} %get-tuple-element.154, f32[4,512]{1,0:T(4,128)S(1)} %get-tuple-element.153), kind=kOutput, calls=%fused_computation.15 | convolution fusion | flops 270794752 | bytes 5251072 | tf_op jit(solution)/shard_map/while/body/eval_jaxpr/mqk,kmd->qmd/dot_general | solution.py:82
  147.7 0.4 copy.44
  148.1 12.2 %all_to_all.66 = bf16[512,4,128]{2,1,0:T(4,128)(2,1)S(1)} all-to-all(bf16[512,4,128]{2,1,0:T(4,128)(2,1)S(1)} %copy.44), channel_id=1, replica_groups=mesh['ctx'=8,'seq'=4] {'ctx'}, dimensions={0} | all-to-all | bytes 1048576 | tf_op jit(solution)/shard_map/all_to_all | solution.py:125
  160.3 0.2 copy.45
  160.5 1.2 reshape.96
  (7 shorter events, 0.1 us)
Async XLA Ops:
  7.2 11.2 %copy-start = (bf16[64,4096]{1,0:T(8,128)(2,1)S(1)}, bf16[64,4096]{1,0:T(8,128)(2,1)}, u32[]{:S(2)}) copy-start(bf16[64,4096]{1,0:T(8,128)(2,1)} %param.10) | copy-start | bytes 1572868
  7.2 11.0 %copy-start.2 = (bf16[64,1024]{1,0:T(8,128)(2,1)S(1)}, bf16[64,1024]{1,0:T(8,128)(2,1)}, u32[]{:S(2)}) copy-start(bf16[64,1024]{1,0:T(8,128)(2,1)} %param.12) | copy-start | bytes 393220
  7.2 11.0 %copy-start.3 = (bf16[64,1024]{1,0:T(8,128)(2,1)S(1)}, bf16[64,1024]{1,0:T(8,128)(2,1)}, u32[]{:S(2)}) copy-start(bf16[64,1024]{1,0:T(8,128)(2,1)} %param.17) | copy-start | bytes 393220
  7.2 45.0 %all-gather.3.cloned.1.call-start = ((), (), s32[]{:S(2)}) async-start(), calls=%async_computation.5 | async-start | bytes 4718592 | tf_op jit(solution)/shard_map/all_gather | solution.py:9
  11.3 102.4 %all-to-all-start.1 = ((bf16[64,32,128]{2,0,1:T(8,128)(2,1)}), bf16[64,32,128]{2,0,1:T(8,128)(2,1)}, u32[]{:S(2)}, u32[]{:S(2)}) async-start(bf16[64,32,128]{2,0,1:T(8,128)(2,1)} %bitcast.10), calls=%async_computation.1 | async-start | bytes 1048576 | tf_op jit(solution)/shard_map/all_to_all | solution.py:121
  16.5 92.9 %all-reduce.2.cloned.1.call-start = ((), (), s32[]{:S(2)}) async-start(), calls=%async_computation.4 | async-start | bytes 524288 | tf_op jit(solution)/shard_map/psum | solution.py:112
  18.8 90.6 %copy-start.1 = (f32[8,128,128]{2,1,0:T(8,128)S(1)}, f32[8,128,128]{2,1,0:T(8,128)}, u32[]{:S(2)}) copy-start(f32[8,128,128]{2,1,0:T(8,128)} %param.13) | copy-start | bytes 1572868
  111.5 6.7 %copy-start.4 = (f32[4096]{0:T(1024)S(1)}, f32[4096]{0:T(1024)}, u32[]{:S(2)}) copy-start(f32[4096]{0:T(1024)} %param.14) | copy-start | bytes 49156
  114.6 13.2 %all-to-all-start.2 = ((bf16[64,32,128]{2,0,1:T(8,128)(2,1)}), bf16[64,32,128]{2,0,1:T(8,128)(2,1)S(1)}, u32[]{:S(2)}, u32[]{:S(2)}) async-start(bf16[64,32,128]{2,0,1:T(8,128)(2,1)} %bitcast.14), calls=%async_computation.2 | async-start | bytes 1048576 | tf_op jit(solution)/shard_map/all_to_all | solution.py:122
  127.8 13.2 %all-to-all-start = ((bf16[64,32,128]{2,0,1:T(8,128)(2,1)}), bf16[64,32,128]{2,0,1:T(8,128)(2,1)S(1)}, u32[]{:S(2)}, u32[]{:S(2)}) async-start(bf16[64,32,128]{2,0,1:T(8,128)(2,1)} %bitcast.95), calls=%async_computation | async-start | bytes 1048576 | tf_op jit(solution)/shard_map/all_to_all | solution.py:118
Sparse Core Ops, SparseCore 0:
  10.5 41.6 all-gather.2
  55.8 53.5 all-reduce.1
where the time goes:
time: 169 us; the launch traced here: 168 us
  waiting for transfers between devices  97.5 us (58%)
  between operations  14.3 us (8%)
  other arithmetic  12.7 us (8%)
  starting transfers between devices  12.2 us (7%)
  blocking collectives  12.2 us (7%)
  matrix products  11.4 us (7%)
  local copies, waits for them, and re-layouts  8.07 us (5%)
    psum x1, waiting for transfers between devices, shards(): lax.psum(local_state.astype(jnp.bfloat16), 'ctx').astype(jnp.float32)  48.4 us
    all_gather x1, waiting for transfers between devices, prefix_2(): pieces = lax.all_gather(value, axis)  33.4 us
    all_to_all x1, blocking collectives, shards(): lax.all_to_all(attended, 'ctx', split_axis=0, concat_axis=1, tiled=True)  12.2 us
    select_n x7, other arithmetic, step(): return jnp.where(position < mine, longer, so_far)  8.58 us
    all_to_all x1, waiting for transfers between devices, shards(): lax.all_to_all(soft_input.reshape(split), 'ctx', split_axis=1, concat_axi...  8.46 us
    all_to_all x1, waiting for transfers between devices, shards(): lax.all_to_all(soft_v, 'ctx', split_axis=1, concat_axis=0, tiled=True)  6.53 us
    all_to_all x1, starting transfers between devices, shards(): lax.all_to_all(soft_k, 'ctx', split_axis=1, concat_axis=0, tiled=True)  5.17 us
    sub x1, matrix products, one_block(): expo = jnp.exp(scores - top)  3.6 us
  transfers between devices with their start and end apart: 5, of which 4 were waited for; matrix products, arithmetic and copies ran while one was open for 12% of the time, Pallas kernels for 0%

commit v1 on v0

--- a/solution.py
+++ b/solution.py
@@ -2,6 +2,22 @@
 import jax.numpy as jnp
 from jax import lax
 from jax.sharding import PartitionSpec as P
+
+
+def swapped_with_each(x, axis, split, join):
+    ways, here = (lax.axis_size(axis), lax.axis_index(axis))
+    width = x.shape[split] // ways
+    shape = list(x.shape)
+    shape[split] = width
+    height = shape[join]
+    shape[join] = height * ways
+    full = jnp.zeros(shape, x.dtype)
+    for mask in range(ways):
+        part = lax.dynamic_slice_in_dim(x, (here ^ mask) * width, width, axis=split)
+        if mask:
+            part = lax.ppermute(part, axis, [(d, d ^ mask) for d in range(ways)])
+        full = lax.dynamic_update_slice_in_dim(full, part, (here ^ mask) * height, axis=join)
+    return full
 
 
 def prefix_2(value, axis, join, neutral):
@@ -118,7 +134,7 @@
             lax.all_to_all(
                 soft_input.reshape(split), "ctx", split_axis=1, concat_axis=0, tiled=True
             ),
-            lax.all_to_all(soft_k, "ctx", split_axis=1, concat_axis=0, tiled=True),
+            swapped_with_each(soft_k, "ctx", 1, 0),
             lax.all_to_all(soft_v, "ctx", split_axis=1, concat_axis=0, tiled=True),
         )
     )

time: 169 us -> 164 us (0.970)
  waiting for transfers between devices: 97.5 us -> 85.3 us
  local copies, waits for them, and re-layouts: 8.07 us -> 12.2 us
  starting transfers between devices: 12.2 us -> 15.4 us
    ppermute x0 -> x7, starting transfers between devices: none -> 7.88 us  [swapped_with_each(): part = lax.ppermute(part, axis, [(d, d ^ mask) for d in range(ways)])]
    all_to_all x1, waiting for transfers between devices: 6.53 us -> 0.01 us  [shards(): lax.all_to_all(soft_v, 'ctx', split_axis=1, concat_axis=0, tiled=True)]
    dynamic_update_slice x0 -> x7, local copies, waits for them, and re-layouts: none -> 6.01 us  [swapped_with_each(): lax.dynamic_update_slice_in_dim(full, part, (here ^ mask) * height, axis=...]
    all_to_all x1 -> x0, starting transfers between devices: 5.17 us -> none  [shards(): lax.all_to_all(soft_k, 'ctx', split_axis=1, concat_axis=0, tiled=True)]
    all_to_all x1, waiting for transfers between devices: 8.46 us -> 5.28 us  [shards(): lax.all_to_all(soft_input.reshape(split), 'ctx', split_axis=1, concat_axi...]
    all_gather x1, waiting for transfers between devices: 33.4 us -> 30.9 us  [prefix_2(): pieces = lax.all_gather(value, axis)]
  transfers between devices with their start and end apart: 5 -> 11, of which waited for: 4 -> 3; matrix products, arithmetic and copies ran while one was open for 12% -> 15% of each run, Pallas kernels for 0% -> 0%
where the time goes in v1:
time: 164 us; the launch traced here: 163 us
  waiting for transfers between devices  85.3 us (52%)
  starting transfers between devices  15.4 us (9%)
  between operations  14.5 us (9%)
  local copies, waits for them, and re-layouts  12.2 us (7%)
  blocking collectives  12.2 us (7%)
  other arithmetic  11.8 us (7%)
  matrix products  11.4 us (7%)
    psum x1, waiting for transfers between devices, shards(): lax.psum(local_state.astype(jnp.bfloat16), 'ctx').astype(jnp.float32)  48.4 us
    all_gather x1, waiting for transfers between devices, prefix_2(): pieces = lax.all_gather(value, axis)  30.9 us
    all_to_all x1, blocking collectives, shards(): lax.all_to_all(attended, 'ctx', split_axis=0, concat_axis=1, tiled=True)  12.2 us
    select_n x7, other arithmetic, step(): return jnp.where(position < mine, longer, so_far)  8.58 us
    ppermute x7, starting transfers between devices, swapped_with_each(): part = lax.ppermute(part, axis, [(d, d ^ mask) for d in range(ways)])  7.88 us
    dynamic_update_slice x7, local copies, waits for them, and re-layouts, swapped_with_each(): lax.dynamic_update_slice_in_dim(full, part, (here ^ mask) * height, axis=...  6.01 us
    all_to_all x1, waiting for transfers between devices, shards(): lax.all_to_all(soft_input.reshape(split), 'ctx', split_axis=1, concat_axi...  5.28 us
    all_to_all x1, starting transfers between devices, shards(): lax.all_to_all(soft_v, 'ctx', split_axis=1, concat_axis=0, tiled=True)  3.95 us
  transfers between devices with their start and end apart: 11, of which 3 were waited for; matrix products, arithmetic and copies ran while one was open for 15% of the time, Pallas kernels for 0%

profile of v1, /device:TPU:0, one launch (start us, length us, event | category | flops | bytes accessed | tf_op | source)
XLA Modules:
  0.0 162.9 jit_solution(12418782325654104759)
XLA Ops:
  7.2 0.0 copy-start
  7.2 0.0 all-gather.3.cloned.1.call-start
  7.3 2.2 %fusion.21 = (bf16[8,128,128]{2,1,0:T(8,128)(2,1)}, f32[8,128,128]{2,1,0:T(8,128)}) fusion(bf16[64,1024]{1,0:T(8,128)(2,1)} %param.12, bf16[64,1024]{1,0:T(8,128)(2,1)} %param.11), kind=kOutput, calls=%fused_computation.55 | convolution fusion | flops 16908288 | bytes 1048576 | tf_op jit(solution)/shard_map/thd,the->hde/dot_general | solution.py:123
  9.5 0.0 all-gather.3.cloned.1.call-update
  9.5 0.9 copy_bitcast_fusion.3
  10.5 0.1 broadcast_in_dim.71
  10.6 0.1 broadcast_in_dim.70
  10.7 0.8 constant_dynamic-slice_fusion
  11.4 0.5 collective-permute-start
  11.9 2.5 %collective-permute-start.1 = (bf16[64,4,128]{2,0,1:T(8,128)(2,1)}, bf16[64,4,128]{2,0,1:T(8,128)(2,1)}, u32[]{:S(2)}, u32[]{:S(2)}) collective-permute-start(bf16[64,4,128]{2,0,1:T(8,128)(2,1)} %get-tuple-element.152), channel_id=1, source_target_pairs={{0,8},{4,12},{8,0},{12,4},{16,24},{20,28},{24,16},{28,20},{1,9},{5... | collective-permute-start | bytes 196616 | tf_op jit(solution)/shard_map/ppermute | solution.py:18
  14.4 0.1 collective-permute-start.2
  14.5 1.7 %collective-permute-start.3 = (bf16[64,4,128]{2,0,1:T(8,128)(2,1)}, bf16[64,4,128]{2,0,1:T(8,128)(2,1)}, u32[]{:S(2)}, u32[]{:S(2)}) collective-permute-start(bf16[64,4,128]{2,0,1:T(8,128)(2,1)} %get-tuple-element.150), channel_id=1, source_target_pairs={{0,16},{4,20},{8,24},{12,28},{16,0},{20,4},{24,8},{28,12},{1,17},{... | collective-permute-start | bytes 196616 | tf_op jit(solution)/shard_map/ppermute | solution.py:18
  16.3 0.0 collective-permute-start.4
  16.3 0.9 broadcast_in_dim.73
  17.2 3.9 %all-to-all-start.1 = ((bf16[64,32,128]{2,0,1:T(8,128)(2,1)}), bf16[64,32,128]{2,0,1:T(8,128)(2,1)S(1)}, u32[]{:S(2)}, u32[]{:S(2)}) async-start(bf16[64,32,128]{2,0,1:T(8,128)(2,1)} %bitcast.11), calls=%async_computation.1 | async-start | bytes 1048576 | tf_op jit(solution)/shard_map/all_to_all | solution.py:138
  21.2 0.0 all-reduce.2.cloned.1.call-start
  21.2 0.7 all-reduce.2.cloned.1.call-update
  22.1 0.1 broadcast_in_dim.65
  22.2 0.4 convolution_multiply_fusion
  22.6 0.1 iota_compare_fusion
  22.7 0.0 collective-permute-done
  22.7 3.0 %collective-permute-start.5 = (bf16[64,4,128]{2,0,1:T(8,128)(2,1)}, bf16[64,4,128]{2,0,1:T(8,128)(2,1)}, u32[]{:S(2)}, u32[]{:S(2)}) collective-permute-start(bf16[64,4,128]{2,0,1:T(8,128)(2,1)} %get-tuple-element.148), channel_id=1, source_target_pairs={{0,24},{4,28},{8,16},{12,20},{16,8},{20,12},{24,0},{28,4},{1,25},{... | collective-permute-start | bytes 196616 | tf_op jit(solution)/shard_map/ppermute | solution.py:18
  25.7 0.9 constant_dynamic-update-slice_fusion.5
  26.6 0.0 collective-permute-done.1
  26.6 0.1 collective-permute-start.6
  26.7 0.9 constant_dynamic-update-slice_fusion.4
  27.5 30.9 %all-gather.3.cloned.1.call-done = f32[64,128,128]{2,1,0:T(8,128)} async-done(((f32[8,128,128]{2,1,0:T(8,128)}), f32[64,128,128]{2,1,0:T(8,128)}) %all-gather.3.cloned.1.call-update) | async-done | bytes 4194320 | tf_op jit(solution)/shard_map/all_gather | solution.py:25
  58.4 8.7 %while.9 = (s32[]{:T(128)}, f32[8,128,128]{2,1,0:T(8,128)S(1)}, s32[]{:T(128)}, f32[8,8,128,128]{3,2,1,0:T(8,128)}, s32[]{:T(128)}, /*index=5*/s32[]{:T(128)}) while((s32[]{:T(128)}, f32[8,128,128]{2,1,0:T(8,128)S(1)}, s32[]{:T(128)}, f32[8,8,128,128]{3,2,1,0:T(8,128)}, s32[]{:T(128)}, /*index=5*/s32[]{:T(128)}) %tuple.59), condition=%wide.region_1.2_spmd.clone, body=%wide.region_0.1_spmd.clone.sunk | while | flops 393220 | bytes 1572957 | solution.py:32
  58.4 1.2 add_select_fusion.2
  59.6 1.2 add_select_fusion.2
  60.9 1.2 add_select_fusion.2
  62.1 1.2 add_select_fusion.2
  63.4 1.2 add_select_fusion.2
  64.6 1.2 add_select_fusion.2
  65.9 1.2 add_select_fusion.2
  67.1 48.4 %all-reduce.2.cloned.1.call-done = bf16[8,128,128]{2,1,0:T(8,128)(2,1)} async-done(((bf16[8,128,128]{2,1,0:T(8,128)(2,1)}), bf16[8,128,128]{2,1,0:T(8,128)(2,1)}) %all-reduce.2.cloned.1.call-update) | async-done | bytes 262160 | tf_op jit(solution)/shard_map/psum | solution.py:128
  115.6 2.0 %convert_add_fusion = (f32[8,128,128]{2,1,0:T(8,128)}, f32[8,128,128]{2,1,0:T(8,128)S(1)}) fusion(f32[8,128,128]{2,1,0:T(8,128)} %param.13, bf16[8,128,128]{2,1,0:T(8,128)(2,1)} %all-reduce.2.cloned.1.call-done, f32[8,128,128]{2,1,0:T(8,128)S(1)} %get-tuple-element.121), kind=kLoop, calls=%fused_computation.26 | loop fusion | flops 393216 | bytes 2359296 | tf_op jit(solution)/shard_map/add | solution.py:128
  117.6 0.2 broadcast_in_dim.64
  117.8 0.0 copy-start.1
  117.8 0.0 copy-start.5
  117.8 1.1 convolution_bitcast_fusion
  119.0 0.1 broadcast_in_dim.68
  119.1 0.9 multiply_reduce_fusion
  120.1 1.1 fusion.10
  121.2 0.9 copy.74
  122.2 0.0 all-to-all-done.1
  122.2 3.5 %all-to-all-start = ((bf16[64,32,128]{2,0,1:T(8,128)(2,1)}), bf16[64,32,128]{2,0,1:T(8,128)(2,1)S(1)}, u32[]{:S(2)}, u32[]{:S(2)}) async-start(bf16[64,32,128]{2,0,1:T(8,128)(2,1)} %bitcast.91), calls=%async_computation | async-start | bytes 1048576 | tf_op jit(solution)/shard_map/all_to_all | solution.py:134
  125.7 0.0 collective-permute-done.2
  125.7 0.9 constant_dynamic-update-slice_fusion.3
  126.5 0.0 collective-permute-done.3
  126.5 0.9 constant_dynamic-update-slice_fusion.2
  127.4 0.0 collective-permute-done.4
  127.4 0.9 constant_dynamic-update-slice_fusion.1
  128.3 0.0 collective-permute-done.5
  128.3 0.9 constant_dynamic-update-slice_fusion
  129.1 0.0 collective-permute-done.6
  129.1 0.9 constant_dynamic-update-slice_fusion.6
  130.1 5.3 %all-to-all-done = bf16[64,32,128]{2,0,1:T(8,128)(2,1)S(1)} async-done(((bf16[64,32,128]{2,0,1:T(8,128)(2,1)}), bf16[64,32,128]{2,0,1:T(8,128)(2,1)S(1)}, u32[]{:S(2)}, u32[]{:S(2)}) %all-to-all-start) | async-done | bytes 524320 | tf_op jit(solution)/shard_map/all_to_all | solution.py:134
  135.4 3.6 %fusion.22 = (f32[4,512]{1,0:T(4,128)S(1)}, f32[4,512,512]{1,2,0:T(8,128)}) fusion(pred[512,512]{0,1:T(8,128)(4,1)S(1)} %iota_compare_fusion, bf16[512,4,128]{2,0,1:T(8,128)(2,1)S(1)} %bitcast.103, bf16[512,4,128]{2,0,1:T(8,128)(2,1)S(1)} %constant_dynamic-update-slice_fusion.6), kind=kOutput, calls=%fused_computation.56 | convolution fusion | flops 272630272 | bytes 5513216 | tf_op jit(solution)/shard_map/while/body/eval_jaxpr/sub | solution.py:96
  139.0 3.1 %fusion.8 = bf16[512,4,128]{2,0,1:T(8,128)(2,1)S(1)} fusion(bf16[512,4,128]{2,0,1:T(8,128)(2,1)S(1)} %bitcast.102, f32[4,512,512]{1,2,0:T(8,128)} %get-tuple-element.162, f32[4,512]{1,0:T(4,128)S(1)} %get-tuple-element.161), kind=kOutput, calls=%fused_computation.15 | convolution fusion | flops 270794752 | bytes 5251072 | tf_op jit(solution)/shard_map/while/body/eval_jaxpr/mqk,kmd->qmd/dot_general | solution.py:98
  142.1 0.4 copy.43
  142.5 12.2 %all_to_all.48 = bf16[512,4,128]{2,1,0:T(4,128)(2,1)S(1)} all-to-all(bf16[512,4,128]{2,1,0:T(4,128)(2,1)S(1)} %copy.43), channel_id=1, replica_groups=mesh['ctx'=8,'seq'=4] {'ctx'}, dimensions={0} | all-to-all | bytes 1048576 | tf_op jit(solution)/shard_map/all_to_all | solution.py:141
  154.7 0.2 copy.44
  154.8 1.2 reshape.96
  (17 shorter events, 0.2 us)
Async XLA Ops:
  7.2 15.1 %copy-start = (bf16[64,4096]{1,0:T(8,128)(2,1)S(1)}, bf16[64,4096]{1,0:T(8,128)(2,1)}, u32[]{:S(2)}) copy-start(bf16[64,4096]{1,0:T(8,128)(2,1)} %param.10) | copy-start | bytes 1572868
  7.2 14.8 %copy-start.2 = (bf16[64,1024]{1,0:T(8,128)(2,1)S(1)}, bf16[64,1024]{1,0:T(8,128)(2,1)}, u32[]{:S(2)}) copy-start(bf16[64,1024]{1,0:T(8,128)(2,1)} %param.11) | copy-start | bytes 393220
  7.2 14.8 %copy-start.3 = (bf16[64,1024]{1,0:T(8,128)(2,1)S(1)}, bf16[64,1024]{1,0:T(8,128)(2,1)}, u32[]{:S(2)}) copy-start(bf16[64,1024]{1,0:T(8,128)(2,1)} %param.12) | copy-start | bytes 393220
  7.2 9.1 %copy-start.4 = (bf16[64,1024]{1,0:T(8,128)(2,1)S(1)}, bf16[64,1024]{1,0:T(8,128)(2,1)}, u32[]{:S(2)}) copy-start(bf16[64,1024]{1,0:T(8,128)(2,1)} %param.17) | copy-start | bytes 393220
  7.2 51.2 %all-gather.3.cloned.1.call-start = ((), (), s32[]{:S(2)}) async-start(), calls=%async_computation.4 | async-start | bytes 4718592 | tf_op jit(solution)/shard_map/all_gather | solution.py:25
  11.4 11.3 %collective-permute-start = (bf16[64,4,128]{2,0,1:T(8,128)(2,1)}, bf16[64,4,128]{2,0,1:T(8,128)(2,1)}, u32[]{:S(2)}, u32[]{:S(2)}) collective-permute-start(bf16[64,4,128]{2,0,1:T(8,128)(2,1)} %get-tuple-element.153), channel_id=1, source_target_pairs={{0,4},{4,0},{8,12},{12,8},{16,20},{20,16},{24,28},{28,24},{1,5},{5... | collective-permute-start | bytes 196616 | tf_op jit(solution)/shard_map/ppermute | solution.py:18
  11.9 14.7 %collective-permute-start.1 = (bf16[64,4,128]{2,0,1:T(8,128)(2,1)}, bf16[64,4,128]{2,0,1:T(8,128)(2,1)}, u32[]{:S(2)}, u32[]{:S(2)}) collective-permute-start(bf16[64,4,128]{2,0,1:T(8,128)(2,1)} %get-tuple-element.152), channel_id=1, source_target_pairs={{0,8},{4,12},{8,0},{12,4},{16,24},{20,28},{24,16},{28,20},{1,9},{5... | collective-permute-start | bytes 196616 | tf_op jit(solution)/shard_map/ppermute | solution.py:18
  14.4 111.3 %collective-permute-start.2 = (bf16[64,4,128]{2,0,1:T(8,128)(2,1)}, bf16[64,4,128]{2,0,1:T(8,128)(2,1)}, u32[]{:S(2)}, u32[]{:S(2)}) collective-permute-start(bf16[64,4,128]{2,0,1:T(8,128)(2,1)} %get-tuple-element.151), channel_id=1, source_target_pairs={{0,12},{4,8},{8,4},{12,0},{16,28},{20,24},{24,20},{28,16},{1,13},{... | collective-permute-start | bytes 196616 | tf_op jit(solution)/shard_map/ppermute | solution.py:18
  14.5 112.0 %collective-permute-start.3 = (bf16[64,4,128]{2,0,1:T(8,128)(2,1)}, bf16[64,4,128]{2,0,1:T(8,128)(2,1)}, u32[]{:S(2)}, u32[]{:S(2)}) collective-permute-start(bf16[64,4,128]{2,0,1:T(8,128)(2,1)} %get-tuple-element.150), channel_id=1, source_target_pairs={{0,16},{4,20},{8,24},{12,28},{16,0},{20,4},{24,8},{28,12},{1,17},{... | collective-permute-start | bytes 196616 | tf_op jit(solution)/shard_map/ppermute | solution.py:18
  16.3 111.1 %collective-permute-start.4 = (bf16[64,4,128]{2,0,1:T(8,128)(2,1)}, bf16[64,4,128]{2,0,1:T(8,128)(2,1)}, u32[]{:S(2)}, u32[]{:S(2)}) collective-permute-start(bf16[64,4,128]{2,0,1:T(8,128)(2,1)} %get-tuple-element.149), channel_id=1, source_target_pairs={{0,20},{4,16},{8,28},{12,24},{16,4},{20,0},{24,12},{28,8},{1,21},{... | collective-permute-start | bytes 196616 | tf_op jit(solution)/shard_map/ppermute | solution.py:18
  17.2 104.9 %all-to-all-start.1 = ((bf16[64,32,128]{2,0,1:T(8,128)(2,1)}), bf16[64,32,128]{2,0,1:T(8,128)(2,1)S(1)}, u32[]{:S(2)}, u32[]{:S(2)}) async-start(bf16[64,32,128]{2,0,1:T(8,128)(2,1)} %bitcast.11), calls=%async_computation.1 | async-start | bytes 1048576 | tf_op jit(solution)/shard_map/all_to_all | solution.py:138
  21.2 94.4 %all-reduce.2.cloned.1.call-start = ((), (), s32[]{:S(2)}) async-start(), calls=%async_computation.3 | async-start | bytes 524288 | tf_op jit(solution)/shard_map/psum | solution.py:128
  22.7 105.5 %collective-permute-start.5 = (bf16[64,4,128]{2,0,1:T(8,128)(2,1)}, bf16[64,4,128]{2,0,1:T(8,128)(2,1)}, u32[]{:S(2)}, u32[]{:S(2)}) collective-permute-start(bf16[64,4,128]{2,0,1:T(8,128)(2,1)} %get-tuple-element.148), channel_id=1, source_target_pairs={{0,24},{4,28},{8,16},{12,20},{16,8},{20,12},{24,0},{28,4},{1,25},{... | collective-permute-start | bytes 196616 | tf_op jit(solution)/shard_map/ppermute | solution.py:18
  26.6 102.6 %collective-permute-start.6 = (bf16[64,4,128]{2,0,1:T(8,128)(2,1)}, bf16[64,4,128]{2,0,1:T(8,128)(2,1)}, u32[]{:S(2)}, u32[]{:S(2)}) collective-permute-start(bf16[64,4,128]{2,0,1:T(8,128)(2,1)} %get-tuple-element.147), channel_id=1, source_target_pairs={{0,28},{4,24},{8,20},{12,16},{16,12},{20,8},{24,4},{28,0},{1,29},{... | collective-permute-start | bytes 196616 | tf_op jit(solution)/shard_map/ppermute | solution.py:18
  117.8 2.2 %copy-start.1 = (bf16[64,4096]{1,0:T(8,128)(2,1)S(1)}, bf16[64,4096]{1,0:T(8,128)(2,1)}, u32[]{:S(2)}) copy-start(bf16[64,4096]{1,0:T(8,128)(2,1)} %param.15) | copy-start | bytes 1572868
  117.8 2.2 %copy-start.5 = (f32[4096]{0:T(1024)S(1)}, f32[4096]{0:T(1024)}, u32[]{:S(2)}) copy-start(f32[4096]{0:T(1024)} %param.14) | copy-start | bytes 49156
  122.2 13.2 %all-to-all-start = ((bf16[64,32,128]{2,0,1:T(8,128)(2,1)}), bf16[64,32,128]{2,0,1:T(8,128)(2,1)S(1)}, u32[]{:S(2)}, u32[]{:S(2)}) async-start(bf16[64,32,128]{2,0,1:T(8,128)(2,1)} %bitcast.91), calls=%async_computation | async-start | bytes 1048576 | tf_op jit(solution)/shard_map/all_to_all | solution.py:134
Sparse Core Ops, SparseCore 0:
  10.5 47.8 all-gather.2
  62.0 53.5 all-reduce.1
